TPU v7x, 256 devices: a whole 4x4x8 slice. The times are simulated.
256 devices in a mesh: dp: 64 (over x, y, z_lo, core), tensor: 4 (over z_hi).
Axes of the slice: x: 4, y: 4, z: 8 (z_hi: 4, z_lo: 2; z = z_hi * 2 + z_lo), core: 2. Of those that a mesh axis runs over, the one named last changes fastest.
Arguments:
- q_nope: bfloat16 [8192, 16384], P('dp', 'tensor'), may hold values from -6 to 6
- q_rope: bfloat16 [8192, 8192], P('dp', 'tensor'), may hold values from -76 to 76
- uk_weight: bfloat16 [512, 16384], P(None, 'tensor'), may hold values from -0.5 to 0.5
- uv_weight: bfloat16 [512, 16384], P(None, 'tensor'), may hold values from -1.5 to 1.5
- prompt_latent: bfloat16 [1024, 512], P('dp'), may hold values from -6 to 6
- prompt_rope: bfloat16 [1024, 64], P('dp'), may hold values from -6 to 6
- doc_latent: bfloat16 [8192, 512], P(('dp', 'tensor')), may hold values from -6 to 6
- doc_rope: bfloat16 [8192, 64], P(('dp', 'tensor')), may hold values from -6 to 6
- doc_lengths: int32 [64], P('dp'), may hold values from 32 to 128, as said below
Outputs:
- attended: bfloat16 [8192, 16384], P('dp', 'tensor')
Inputs may be any that keep to these rules, and one draw needn't show every extreme that they name: `doc_lengths`: lengths lie between 32 and 128; tokens of a document at or past its length are padding.
All inputs are finite; a program needn't handle non-finite values.
Results may differ from a plain program's by a relative error of at most 0.0085.
Values may be sent and summed in bfloat16 or wider, within the bound.
A program may use at most 128 MiB of HBM per device.

v0:
```python
import jax
import jax.numpy as jnp
from jax import lax
from jax.sharding import PartitionSpec as P

DN = 128
DR = 64
DV = 128
LAT = 512


def per_device(
    q_nope,
    q_rope,
    uk_weight,
    uv_weight,
    prompt_latent,
    prompt_rope,
    doc_latent,
    doc_rope,
    doc_lengths,
):
    row_count = q_nope.shape[0]
    head_count = q_nope.shape[1] // DN
    doc_count = doc_lengths.shape[0]
    doc_span = row_count // doc_count
    scaling = (DN + DR) ** (-0.5)
    query_nope = q_nope.reshape(row_count, head_count, DN)
    query_rope = q_rope.reshape(row_count, head_count, DR)
    query_lat = jnp.einsum(
        "thd,lhd->thl",
        query_nope,
        uk_weight.reshape(LAT, head_count, DN),
        preferred_element_type=jnp.float32,
    ).astype(jnp.bfloat16)
    own_latent, own_rope = (
        lax.all_gather(doc_latent, "tensor", axis=0, tiled=True),
        lax.all_gather(doc_rope, "tensor", axis=0, tiled=True),
    )
    position = jnp.arange(doc_span)
    causal = position[:, None] >= position[None, :]
    is_valid = (position[None, :] < doc_lengths[:, None]).reshape(row_count)
    latent_docs = own_latent.reshape(doc_count, doc_span, LAT)
    rope_docs = own_rope.reshape(doc_count, doc_span, DR)
    doc_scores = (
        jnp.einsum(
            "dqhl,dkl->dqhk",
            query_lat.reshape(doc_count, doc_span, head_count, LAT),
            latent_docs,
            preferred_element_type=jnp.float32,
        )
        + jnp.einsum(
            "dqhr,dkr->dqhk",
            query_rope.reshape(doc_count, doc_span, head_count, DR),
            rope_docs,
            preferred_element_type=jnp.float32,
        )
    ) * scaling
    doc_scores = jnp.where(causal[None, :, None, :], doc_scores, -jnp.inf)
    row_max = jnp.max(doc_scores, axis=3)
    weights = jnp.exp(doc_scores - row_max[..., None])
    summed = jnp.sum(weights, axis=3)
    gathered = jnp.einsum(
        "dqhk,dkl->dqhl",
        weights.astype(jnp.bfloat16),
        latent_docs,
        preferred_element_type=jnp.float32,
    )
    run_max = row_max.reshape(row_count, head_count)
    run_sum = summed.reshape(row_count, head_count)
    run_acc = gathered.reshape(row_count, head_count, LAT)
    latent_rows = lax.all_gather(prompt_latent, "dp", axis=0, tiled=True)
    rope_rows = lax.all_gather(prompt_rope, "dp", axis=0, tiled=True)
    piece_scores = (
        jnp.einsum("thl,kl->thk", query_lat, latent_rows, preferred_element_type=jnp.float32)
        + jnp.einsum("thr,kr->thk", query_rope, rope_rows, preferred_element_type=jnp.float32)
    ) * scaling
    new_max = jnp.maximum(run_max, jnp.max(piece_scores, axis=2))
    rescale = jnp.exp(run_max - new_max)
    piece_weights = jnp.exp(piece_scores - new_max[..., None])
    new_sum = run_sum * rescale + jnp.sum(piece_weights, axis=2)
    new_acc = run_acc * rescale[..., None] + jnp.einsum(
        "thk,kl->thl",
        piece_weights.astype(jnp.bfloat16),
        latent_rows,
        preferred_element_type=jnp.float32,
    )
    out_lat = (new_acc / new_sum[..., None]).astype(jnp.bfloat16)
    projected = jnp.einsum(
        "thl,lhv->thv",
        out_lat,
        uv_weight.reshape(LAT, head_count, DV),
        preferred_element_type=jnp.float32,
    )
    projected = jnp.where(is_valid[:, None, None], projected, 0.0).astype(jnp.bfloat16)
    return projected.reshape(row_count, head_count * DV)


def solution(mesh):
    return jax.shard_map(
        per_device,
        mesh=mesh,
        in_specs=(
            P("dp", "tensor"),
            P("dp", "tensor"),
            P(None, "tensor"),
            P(None, "tensor"),
            P("dp", None),
            P("dp", None),
            P(("dp", "tensor"), None),
            P(("dp", "tensor"), None),
            P("dp"),
        ),
        out_specs=P("dp", "tensor"),
        check_vma=False,
    )
```

profile of v0, /device:TPU:1, one launch (start us, length us, event | category | flops | bytes accessed | tf_op | source)
XLA Modules:
  0.0 183.9 jit_solution(1882868323576917431)
XLA Ops:
  6.5 0.0 copy-start
  6.5 0.0 all-gather.2.cloned.1.call-start
  6.5 0.7 all-gather.2.cloned.1.call-update
  7.3 1.3 copy.21
  8.6 85.3 %all_gather.15 = bf16[1024,64]{1,0:T(8,128)(2,1)S(1)} all-gather(bf16[16,64]{1,0:T(8,128)(2,1)} %param.14), channel_id=1, replica_groups=mesh['dp'=64,'tensor'=4] {'dp'}, dimensions={0}, use_global_device_ids=true | all-gather | bytes 133120 | tf_op jit(solution)/shard_map/all_gather | solution.py:73
  93.9 0.0 copy-start.5
  93.9 0.0 copy-start.4
  93.9 6.5 %copy.27 = bf16[512,4096]{0,1:T(8,128)(2,1)} copy(bf16[512,4096]{1,0:T(8,128)(2,1)} %param.12) | data formatting | bytes 8388608 | tf_op jit(solution)/shard_map/reshape | solution.py:92
  101.1 0.0 copy-done.5
  101.1 13.7 %all_gather.13 = bf16[128,64]{1,0:T(8,128)(2,1)S(1)} all-gather(bf16[32,64]{1,0:T(8,128)(2,1)S(1)} %copy-done.5), channel_id=1, replica_groups=mesh['dp'=64,'tensor'=4] {'tensor'}, dimensions={0}, use_global_device_ids=true | all-gather | bytes 20480 | tf_op jit(solution)/shard_map/all_gather | solution.py:38
  114.8 0.0 copy-done.4
  114.8 11.1 %all_gather.12 = bf16[128,512]{1,0:T(8,128)(2,1)S(1)} all-gather(bf16[32,512]{1,0:T(8,128)(2,1)S(1)} %copy-done.4), channel_id=1, replica_groups=mesh['dp'=64,'tensor'=4] {'tensor'}, dimensions={0}, use_global_device_ids=true | all-gather | bytes 163840 | tf_op jit(solution)/shard_map/all_gather | solution.py:37
  125.8 0.4 fusion.37
  126.2 0.0 copy-done
  126.3 3.4 %fusion.17 = bf16[32,512,128]{2,1,0:T(8,128)(2,1)S(1)} fusion(bf16[512,4096]{1,0:T(8,128)(2,1)} %param.11, bf16[128,4096]{1,0:T(8,128)(2,1)S(1)} %copy-done), kind=kOutput, calls=%fused_computation.15 | convolution fusion | flops 538968064 | bytes 9437184 | tf_op jit(solution)/shard_map/thd,lhd->thl/dot_general | solution.py:30
  129.7 0.0 copy-start.3
  129.7 0.9 fusion.39
  130.6 1.0 copy-done.3
  131.7 0.4 fusion.20
  132.1 4.5 %fusion.26 = f32[128,32,512]{2,0,1:T(8,128)} fusion(f32[128,32,128]{0,2,1:T(8,128)S(1)} %get-tuple-element.8, f32[128,32]{0,1:T(8,128)S(1)} %get-tuple-element.7, bf16[128,512]{1,0:T(8,128)(2,1)S(1)} %all_gather.12), kind=kOutput, calls=%fused_computation.21 | convolution fusion | flops 537919488 | bytes 10633216 | tf_op jit(solution)/shard_map/dqhk,dkl->dqhl/dot_general | solution.py:63
  136.6 0.0 all-gather.2.cloned.1.call-done
  136.6 12.8 %fusion.8 = f32[128,32,1024]{2,0,1:T(8,128)} fusion(bf16[32,512,128]{2,1,0:T(8,128)(2,1)} %copy-done.3, bf16[1024,512]{1,0:T(8,128)(2,1)} %all-gather.2.cloned.1.call-done), kind=kOutput, calls=%fused_computation.10 | convolution fusion | flops 4294967296 | bytes 22020096 | tf_op jit(solution)/shard_map/thl,kl->thk/dot_general | solution.py:75
  149.4 7.2 %fusion.40 = (f32[128,32]{0,1:T(8,128)S(1)}, f32[128,32,1024]{2,0,1:T(8,128)S(1)}) fusion(f32[128,32,1024]{2,0,1:T(8,128)} %fusion.8, bf16[128,32,64]{0,2,1:T(8,128)(2,1)S(1)} %bitcast.57, bf16[1024,64]{1,0:T(8,128)(2,1)S(1)} %all_gather.15), kind=kOutput, calls=%fused_computation.37 | convolution fusion | flops 549449728 | bytes 34226176 | tf_op jit(solution)/shard_map/thr,kr->thk/dot_general | solution.py:76
  156.6 0.0 copy-start.2
  156.6 0.0 copy-start.6
  156.6 3.8 %fusion = f32[128,32]{0,1:T(8,128)S(1)} fusion(f32[128,32,1024]{2,0,1:T(8,128)S(1)} %get-tuple-element.10, f32[128,32]{0,1:T(8,128)S(1)} %max.13), kind=kLoop, calls=%fused_computation.2 | loop fusion | flops 8384512 | bytes 16809984 | tf_op jit(solution)/shard_map/reduce_sum | solution.py:81
  160.4 2.1 %copy-done.2 = f32[128,32,1024]{2,0,1:T(8,128)} copy-done((f32[128,32,1024]{2,0,1:T(8,128)}, f32[128,32,1024]{2,0,1:T(8,128)S(1)}, u32[]{:S(2)}) %copy-start.2) | copy-done | bytes 16777240
  162.5 0.0 copy-done.6
  162.5 0.0 copy-start.1
  162.5 13.2 %select_convert_fusion = bf16[32,128,128]{1,2,0:T(8,128)(2,1)S(1)} fusion(bf16[512,32,128]{0,2,1:T(8,128)(2,1)} %bitcast.58, f32[128,32,512]{2,0,1:T(8,128)} %fusion.26, f32[128,32]{0,1:T(8,128)S(1)} %get-tuple-element.5, f32[128,32]{0,1:T(8,128)S(1)} %get-tuple-element.6, f32[128,32,1024]{2,0,1:T(8,128)} %copy-done.2, f32[128,32]{0,1:T(8,128)S(1)} %max.13, ...), kind=kOutput, calls=%fused_computation.16 | convolution fusion | flops 4849664000 | bytes 31506560 | tf_op jit(solution)/shard_map/thl,lhv->thv/dot_general | solution.py:89
  175.8 1.3 copy.24
  177.1 0.0 copy-done.1
  (4 shorter events, 0.0 us)
Async XLA Ops:
  6.5 119.7 %copy-start = (bf16[128,4096]{1,0:T(8,128)(2,1)S(1)}, bf16[128,4096]{1,0:T(8,128)(2,1)}, u32[]{:S(2)}) copy-start(bf16[128,4096]{1,0:T(8,128)(2,1)} %param.9) | copy-start | bytes 3145732
  6.5 130.0 %all-gather.2.cloned.1.call-start = ((), (), s32[]{:S(2)}) async-start(), calls=%async_computation | async-start | bytes 1064960 | tf_op jit(solution)/shard_map/all_gather | solution.py:72
  93.9 7.2 %copy-start.5 = (bf16[32,64]{1,0:T(8,128)(2,1)S(1)}, bf16[32,64]{1,0:T(8,128)(2,1)}, u32[]{:S(2)}) copy-start(bf16[32,64]{1,0:T(8,128)(2,1)} %param.16) | copy-start | bytes 12292
  93.9 20.9 %copy-start.4 = (bf16[32,512]{1,0:T(8,128)(2,1)S(1)}, bf16[32,512]{1,0:T(8,128)(2,1)}, u32[]{:S(2)}) copy-start(bf16[32,512]{1,0:T(8,128)(2,1)} %param.15) | copy-start | bytes 98308
  129.7 2.0 %copy-start.3 = (bf16[32,512,128]{2,1,0:T(8,128)(2,1)}, bf16[32,512,128]{2,1,0:T(8,128)(2,1)S(1)}, u32[]{:S(2)}) copy-start(bf16[32,512,128]{2,1,0:T(8,128)(2,1)S(1)} %fusion.17) | copy-start | bytes 12582916
  156.6 5.9 %copy-start.2 = (f32[128,32,1024]{2,0,1:T(8,128)}, f32[128,32,1024]{2,0,1:T(8,128)S(1)}, u32[]{:S(2)}) copy-start(f32[128,32,1024]{2,0,1:T(8,128)S(1)} %get-tuple-element.10) | copy-start | bytes 50331652
  156.6 5.9 %copy-start.6 = (bf16[1024,512]{1,0:T(8,128)(2,1)S(1)}, bf16[1024,512]{1,0:T(8,128)(2,1)}, u32[]{:S(2)}) copy-start(bf16[1024,512]{1,0:T(8,128)(2,1)} %all-gather.2.cloned.1.call-done) | copy-start | bytes 3145732
  162.5 14.6 %copy-start.1 = (bf16[128,4096]{1,0:T(8,128)(2,1)S(1)}, bf16[128,4096]{1,0:T(8,128)(2,1)}, u32[]{:S(2)}) copy-start(bf16[128,4096]{1,0:T(8,128)(2,1)} %param.9) | copy-start | bytes 3145732
Sparse Core Ops, SparseCore 0:
  9.2 108.1 all-gather.1
where the time goes:
time: 187 us; the launch traced here: 184 us
  blocking collectives  110 us (59%)
  matrix products  42.5 us (23%)
  between operations  14.2 us (8%)
  local copies, waits for them, and re-layouts  12.3 us (7%)
  other arithmetic  4.21 us (2%)
    all_gather x1, blocking collectives, per_device(): rope_rows = lax.all_gather(prompt_rope, 'dp', axis=0, tiled=True)  85.3 us
    all_gather x1, blocking collectives, per_device(): lax.all_gather(doc_rope, 'tensor', axis=0, tiled=True)  13.7 us
    dot_general x1, matrix products, per_device(): jnp.einsum('thl,lhv->thv', out_lat, uv_weight.reshape(LAT, head_count, DV...  13.2 us
    dot_general x1, matrix products, per_device(): jnp.einsum('thl,kl->thk', query_lat, latent_rows, preferred_element_type=...  12.8 us
    all_gather x1, blocking collectives, per_device(): lax.all_gather(doc_latent, 'tensor', axis=0, tiled=True)  11.1 us
    dot_general x1, matrix products, per_device(): jnp.einsum('thr,kr->thk', query_rope, rope_rows, preferred_element_type=j...  7.18 us
    reshape x1, local copies, waits for them, and re-layouts, per_device(): uv_weight.reshape(LAT, head_count, DV)  6.5 us
    dot_general x1, matrix products, per_device(): jnp.einsum('dqhk,dkl->dqhl', weights.astype(jnp.bfloat16), latent_docs, p...  4.52 us
  transfers between devices with their start and end apart: 1, of which 0 were waited for; matrix products, arithmetic and copies ran while one was open for 10% of the time, Pallas kernels for 0%

commit v1 on v0

v1 whole, which is shorter than its diff:
```python
import functools

import jax
import jax.numpy as jnp
from jax import lax
from jax.experimental import pallas as pl
from jax.experimental.pallas import tpu as pltpu
from jax.sharding import PartitionSpec as P

MESH = pl.DeviceIdType.MESH
F32, BF16 = jnp.float32, jnp.bfloat16

DN = 128
DR = 64
DV = 128
LAT = 512
WIDE = 640
TOK = 128
HEADS = 32
GROUP = 4
N = GROUP * TOK
GROUPS = HEADS // GROUP
PROMPT = 1024
KEYS = PROMPT + TOK
SCALE = (DN + DR) ** -0.5 * 1.4426950408889634


def dot(a, b):
    return jnp.dot(a, b, preferred_element_type=F32)


def kernel(
    qn_h, qr_h, uk_h, uv_h, pl_h, pr_h, dl_h, dr_h, ln,
    out_h,
    qn, qr, uk, uv, pls, prs, dls, drs,
    keys, docs, ct, qt, s0, s1, p0, p1, mx, inv, out_v,
    lsem, osem, ssem, rsem,
):
    S, PR = (s0, s1), (p0, p1)
    me = lax.axis_index("dp")
    ten = lax.axis_index("tensor")
    x, y, zl, c = me // 16, (me // 4) % 4, (me // 2) % 2, me % 2
    a = c * x + (1 - c) * y
    b = c * y + (1 - c) * x
    g = a * 2 + zl

    def place(b_, g_):
        a_, z_ = g_ // 2, g_ % 2
        x_ = c * a_ + (1 - c) * b_
        y_ = c * b_ + (1 - c) * a_
        return (x_ * 16 + y_ * 4 + z_ * 2 + c, ten)

    near = [place(b, (g + d) % 8) for d in range(1, 8)]
    up, down = place((b + 1) % 4, g), place((b + 3) % 4, g)
    twin = (me + 1 - 2 * c, ten)
    others = [(me, (ten + d) % 4) for d in range(1, 4)]

    loads = {}

    def load(name, src, dst, k):
        loads[name] = pltpu.make_async_copy(src, dst, lsem.at[k])
        loads[name].start()

    load("pl", pl_h, pls, 0)
    load("pr", pr_h, prs, 1)
    load("dl", dl_h, dls, 2)
    load("dr", dr_h, drs, 3)
    load("qn", qn_h, qn, 4)
    load("qr", qr_h, qr, 5)
    for j in range(4):
        load("uk%d" % j, uk_h.at[:, pl.ds(j * 1024, 1024)], uk.at[:, pl.ds(j * 1024, 1024)], 6 + j)
    load("uv", uv_h, uv, 10)

    barrier = pltpu.get_barrier_semaphore()
    peers = near + [up, down, twin] + others
    for peer in peers:
        pl.semaphore_signal(barrier, inc=1, device_id=peer, device_id_type=MESH)

    for name in ("pl", "pr", "dl", "dr"):
        loads[name].wait()
    keys[c, b, g, :, :LAT] = pls[...]
    keys[c, b, g, :, LAT:] = jnp.concatenate([prs[...], jnp.zeros((16, DR), BF16)], axis=1)
    docs[ten, :, :LAT] = dls[...]
    docs[ten, :, LAT:] = jnp.concatenate([drs[...], jnp.zeros((32, DR), BF16)], axis=1)
    pl.semaphore_wait(barrier, len(peers))

    count = [0]
    sent = []

    def send(ref, peer):
        k = count[0]
        count[0] += 1
        copy = pltpu.make_async_remote_copy(
            src_ref=ref, dst_ref=ref, send_sem=ssem.at[k], recv_sem=rsem.at[k], device_id=peer, device_id_type=MESH
        )
        copy.start()
        sent.append(copy)
        return copy

    first = [send(keys.at[c, b, g], peer) for peer in near]
    doc = [send(docs.at[ten], peer) for peer in others]

    def qlat(i, _):
        zero = jnp.zeros((TOK, TOK), BF16)
        for p in range(GROUP // 2):
            cols = pl.ds(pl.multiple_of(i * N + p * 256, 256), 256)
            q = qn[:, cols]
            diag = jnp.concatenate(
                [
                    jnp.concatenate([q[:, :DN].T, zero], axis=1),
                    jnp.concatenate([zero, q[:, DN:].T], axis=1),
                ],
                axis=0,
            )
            qt[i, :LAT, p * 256 : (p + 1) * 256] = dot(uk[:, cols], diag).astype(BF16)
            r = qr[:, pl.ds(pl.multiple_of(i * (N // 2) + p * 128, 128), 128)].T
            qt[i, LAT : LAT + DR, p * 256 : (p + 1) * 256] = jnp.concatenate([r[:DR], r[DR:]], axis=1)
        qt[i, LAT + DR :, :] = jnp.zeros((WIDE - LAT - DR, N), BF16)
        return 0

    loads["qn"].wait()
    loads["qr"].wait()
    loads["uk0"].wait()
    lax.fori_loop(0, 2, qlat, 0)

    for copy in first:
        copy.wait_recv()
    lo, hi = pl.ds(0, 4), pl.ds(4, 4)
    up0 = send(keys.at[c, b, lo], up)
    down1 = send(keys.at[c, b, hi], down)
    up1 = send(keys.at[c, b, hi], up)
    down0 = send(keys.at[c, b, lo], down)
    own = send(keys.at[c, b], twin)

    loads["uk1"].wait()
    lax.fori_loop(2, 4, qlat, 0)

    prev, nxt, far = (b + 3) % 4, (b + 1) % 4, (b + 2) % 4
    up0.wait_recv()
    far0 = send(keys.at[c, prev, lo], up)
    down1.wait_recv()
    far1 = send(keys.at[c, nxt, hi], down)
    up1.wait_recv()
    t0 = send(keys.at[c, prev], twin)
    down0.wait_recv()
    t1 = send(keys.at[c, nxt], twin)

    loads["uk2"].wait()
    loads["uk3"].wait()
    lax.fori_loop(4, 8, qlat, 0)

    far0.wait_recv()
    t2 = send(keys.at[c, far, lo], twin)
    far1.wait_recv()
    t3 = send(keys.at[c, far, hi], twin)
    for copy in doc:
        copy.wait_recv()
    for copy in (own, t0, t1, t2, t3):
        copy.wait_recv()
    for copy in sent:
        copy.wait_send()

    for j in range(8):
        ct[:, j * 128 : (j + 1) * 128] = keys[j // 4, j % 4].reshape(128, WIDE)[:, :LAT].T
    ct[:, PROMPT:] = docs[...].reshape(128, WIDE)[:, :LAT].T
    loads["uv"].wait()

    key_at = lax.broadcasted_iota(jnp.int32, (TOK, TOK), 0)
    tok_at = lax.broadcasted_iota(jnp.int32, (TOK, TOK), 1)
    causal = jnp.concatenate([key_at <= tok_at] * GROUP, axis=1)
    valid = key_at < ln[0]

    def scores(i, k):
        top = None
        for j in range(0, KEYS, 256):
            if j < PROMPT:
                block = keys[j // 512, (j // 128) % 4 : (j // 128) % 4 + 2].reshape(256, WIDE)
                s = dot(block, qt[i])
            else:
                s = dot(docs[...].reshape(TOK, WIDE), qt[i])
                s = jnp.where(causal, s, -1e30)
            rows = s.shape[0]
            S[k][j : j + rows] = s
            m = jnp.max(s.reshape(rows // 8, 8, N), axis=0)
            top = m if top is None else jnp.maximum(top, m)
            yield
        mx[k] = jnp.broadcast_to(jnp.max(top, axis=0, keepdims=True) * SCALE, (8, N))
        yield

    def weights(k):
        m = mx[k][:1]
        total = jnp.zeros((8, N), F32)
        for r in range(0, KEYS, 64):
            w = jnp.exp2(S[k][r : r + 64] * SCALE - m)
            total = total + jnp.sum(w.reshape(8, 8, N), axis=0)
            PR[k][r : r + 64] = w.astype(BF16)
            yield
        inv[k] = jnp.broadcast_to(1.0 / jnp.sum(total, axis=0, keepdims=True), (8, N))
        yield

    def project(i, k):
        o = (dot(ct[...], PR[k][...]) * inv[k][:1]).astype(BF16)
        yield
        for h in range(GROUP):
            cols = pl.ds(pl.multiple_of(i * N + h * DV, DV), DV)
            v = lax.dot_general(
                o[:, h * TOK : (h + 1) * TOK], uv[:, cols], (((0,), (0,)), ((), ())), preferred_element_type=F32
            )
            out_v[:, cols] = jnp.where(valid, v, 0.0).astype(BF16)
            yield
        cols = pl.ds(pl.multiple_of(i * N, N), N)
        pltpu.make_async_copy(out_v.at[:, cols], out_h.at[:, cols], osem.at[i]).start()
        yield

    def run(*steps):
        most = max(n for _, n in steps)
        done = [0] * len(steps)
        for t in range(1, most + 1):
            for k, (step, n) in enumerate(steps):
                while done[k] * most < t * n and done[k] < n:
                    next(step, None)
                    done[k] += 1
        for step, _ in steps:
            for _ in step:
                pass

    def A(i, k):
        return scores(i, k), 6

    def B(k):
        return weights(k), 19

    def C(i, k):
        return project(i, k), GROUP + 2

    run(A(0, 0))
    run(A(1, 1), B(0))

    def body(t, _):
        i = 2 * t + 1
        run(C(i - 1, 0), A(i + 1, 0), B(1))
        run(C(i, 1), A(jnp.minimum(i + 2, GROUPS - 1), 1), B(0))
        return 0

    lax.fori_loop(0, GROUPS // 2 - 1, body, 0)
    run(C(GROUPS - 2, 0), B(1))
    run(C(GROUPS - 1, 1))
    for i in range(GROUPS):
        cols = pl.ds(i * N, N)
        pltpu.make_async_copy(out_v.at[:, cols], out_h.at[:, cols], osem.at[i]).wait()


def per_device(q_nope, q_rope, uk_weight, uv_weight, prompt_latent, prompt_rope, doc_latent, doc_rope, doc_lengths):
    hbm = pl.BlockSpec(memory_space=pl.ANY)
    copies = 20
    return pl.pallas_call(
        kernel,
        out_shape=jax.ShapeDtypeStruct((TOK, HEADS * DV), BF16),
        in_specs=[hbm] * 8 + [pl.BlockSpec(memory_space=pltpu.SMEM)],
        out_specs=hbm,
        scratch_shapes=[
            pltpu.VMEM((TOK, HEADS * DN), BF16),
            pltpu.VMEM((TOK, HEADS * DR), BF16),
            pltpu.VMEM((LAT, HEADS * DN), BF16),
            pltpu.VMEM((LAT, HEADS * DV), BF16),
            pltpu.VMEM((16, LAT), BF16),
            pltpu.VMEM((16, DR), BF16),
            pltpu.VMEM((32, LAT), BF16),
            pltpu.VMEM((32, DR), BF16),
            pltpu.VMEM((2, 4, 8, 16, WIDE), BF16),
            pltpu.VMEM((4, 32, WIDE), BF16),
            pltpu.VMEM((LAT, KEYS), BF16),
            pltpu.VMEM((GROUPS, WIDE, N), BF16),
            pltpu.VMEM((KEYS, N), F32),
            pltpu.VMEM((KEYS, N), F32),
            pltpu.VMEM((KEYS, N), BF16),
            pltpu.VMEM((KEYS, N), BF16),
            pltpu.VMEM((2, 8, N), F32),
            pltpu.VMEM((2, 8, N), F32),
            pltpu.VMEM((TOK, HEADS * DV), BF16),
            pltpu.SemaphoreType.DMA((11,)),
            pltpu.SemaphoreType.DMA((GROUPS,)),
            pltpu.SemaphoreType.DMA((24,)),
            pltpu.SemaphoreType.DMA((24,)),
        ],
        compiler_params=pltpu.CompilerParams(
            collective_id=0, has_side_effects=True, vmem_limit_bytes=56 * 2**20
        ),
        name="attend",
    )(q_nope, q_rope, uk_weight, uv_weight, prompt_latent, prompt_rope, doc_latent, doc_rope, doc_lengths)


def solution(mesh):
    return jax.shard_map(
        per_device,
        mesh=mesh,
        in_specs=(
            P("dp", "tensor"),
            P("dp", "tensor"),
            P(None, "tensor"),
            P(None, "tensor"),
            P("dp", None),
            P("dp", None),
            P(("dp", "tensor"), None),
            P(("dp", "tensor"), None),
            P("dp"),
        ),
        out_specs=P("dp", "tensor"),
        check_vma=False,
    )
```

time: 187 us -> 47 us (0.25); the launches traced: 184 us -> 46.9 us
  blocking collectives: 110 us -> 0 us
  Pallas kernels: 0 us -> 43.9 us
  matrix products: 42.5 us -> 0 us
  between operations: 14.2 us -> 0.66 us
  local copies, waits for them, and re-layouts: 12.3 us -> 2.29 us
  other arithmetic: 4.21 us -> 0 us
    all_gather x3 -> x0, blocking collectives: 110 us -> none  [the longest x1 85.3 us: per_device(): rope_rows = lax.all_gather(prompt_rope, 'dp', axis=0, tiled=True)]
    pallas_call x0 -> x1, Pallas kernels: none -> 43.9 us  [per_device(): pl.pallas_call(kernel, out_shape=jax.ShapeDtypeStruct((TOK, HEADS * DV),...]
    dot_general x7 -> x0, matrix products: 42.5 us -> none  [the longest x1 13.2 us: per_device(): jnp.einsum('thl,lhv->thv', out_lat, uv_weight.reshape(LAT, head_count, DV...]
    reshape x2 -> x0, local copies, waits for them, and re-layouts: 7.81 us -> none  [the longest x1 6.5 us: per_device(): uv_weight.reshape(LAT, head_count, DV)]
    reduce_sum x2 -> x0, other arithmetic: 4.18 us -> none  [the longest x1 3.79 us: per_device(): new_sum = run_sum * rescale + jnp.sum(piece_weights, axis=2)]
    unnamed x15 -> x1, local copies, waits for them, and re-layouts: 4.46 us -> 2.29 us
  transfers between devices with their start and end apart: 1 -> 0, of which waited for: 0 -> 0; matrix products, arithmetic and copies ran while one was open for 10% -> 0% of each run, Pallas kernels for 0% -> 0%
where the time goes in v1:
time: 47 us; the launch traced here: 46.9 us
  Pallas kernels  43.9 us (93%)
  local copies, waits for them, and re-layouts  2.29 us (5%)
  between operations  0.66 us (1%)
    pallas_call x1, Pallas kernels, per_device(): pl.pallas_call(kernel, out_shape=jax.ShapeDtypeStruct((TOK, HEADS * DV),...  43.9 us
    unnamed x1, local copies, waits for them, and re-layouts  2.29 us

profile of v1, /device:TPU:1, one launch (start us, length us, event | category | flops | bytes accessed | tf_op | source)
XLA Modules:
  0.0 46.9 jit_solution(15085596891898497152)
XLA Ops:
  0.7 43.9 %attend.1 = bf16[128,4096]{1,0:T(8,128)(2,1)} custom-call(bf16[128,4096]{1,0:T(8,128)(2,1)} %qn_h.1, bf16[128,2048]{1,0:T(8,128)(2,1)} %qr_h.1, bf16[512,4096]{1,0:T(8,128)(2,1)} %uk_h.1, bf16[512,4096]{1,0:T(8,128)(2,1)} %uv_h.1, bf16[16,512]{1,0:T(8,128)(2,1)} %pl_h.1, bf16[16,64]{1,0:T(8,128)(2,1)} %pr_h.1, bf16[32,512]{1,0:T(8,128)(2,1)} %dl_h.1, ...), custom_call_target="tpu_custom_call" | custom-call | tf_op jit(solution)/shard_map/attend/pallas_call | solution.py:256
  44.6 2.3 %copy.12 = bf16[128,4096]{1,0:T(8,128)(2,1)} copy(bf16[128,4096]{1,0:T(8,128)(2,1)} %attend.1) | data formatting | bytes 2097152

commit v2 on v1

--- a/solution.py
+++ b/solution.py
@@ -33,7 +33,7 @@
     qn_h, qr_h, uk_h, uv_h, pl_h, pr_h, dl_h, dr_h, ln,
     out_h,
     qn, qr, uk, uv, pls, prs, dls, drs,
-    keys, docs, ct, qt, s0, s1, p0, p1, mx, inv, out_v,
+    keys, docs, ct, qt, s0, s1, p0, p1, mx, al, sm, acc, mrun, lrun, out_v,
     lsem, osem, ssem, rsem,
 ):
     S, PR = (s0, s1), (p0, p1)
@@ -48,11 +48,16 @@
         a_, z_ = g_ // 2, g_ % 2
         x_ = c * a_ + (1 - c) * b_
         y_ = c * b_ + (1 - c) * a_
-        return (x_ * 16 + y_ * 4 + z_ * 2 + c, ten)
-
-    near = [place(b, (g + d) % 8) for d in range(1, 8)]
-    up, down = place((b + 1) % 4, g), place((b + 3) % 4, g)
-    twin = (me + 1 - 2 * c, ten)
+        return x_ * 16 + y_ * 4 + z_ * 2 + c
+
+    flip = 1 - 2 * c
+    near = [(place(b, (g + d) % 8), ten) for d in range(1, 8)]
+    up_at, down_at = place((b + 1) % 4, g), place((b + 3) % 4, g)
+    up, down = (up_at, ten), (down_at, ten)
+    up_twin, down_twin = (up_at + flip, ten), (down_at + flip, ten)
+    v_up = (c * ((x + 1) % 4) + (1 - c) * x) * 16 + (c * y + (1 - c) * ((y + 1) % 4)) * 4 + zl * 2 + (1 - c)
+    v_down = (c * ((x + 3) % 4) + (1 - c) * x) * 16 + (c * y + (1 - c) * ((y + 3) % 4)) * 4 + zl * 2 + (1 - c)
+    twin = (me + flip, ten)
     others = [(me, (ten + d) % 4) for d in range(1, 4)]
 
     loads = {}
@@ -72,7 +77,7 @@
     load("uv", uv_h, uv, 10)
 
     barrier = pltpu.get_barrier_semaphore()
-    peers = near + [up, down, twin] + others
+    peers = near + [up, down, up_twin, down_twin, (v_up, ten), (v_down, ten), twin] + others
     for peer in peers:
         pl.semaphore_signal(barrier, inc=1, device_id=peer, device_id_type=MESH)
 
@@ -120,97 +125,14 @@
 
     loads["qn"].wait()
     loads["qr"].wait()
-    loads["uk0"].wait()
-    lax.fori_loop(0, 2, qlat, 0)
-
-    for copy in first:
-        copy.wait_recv()
-    lo, hi = pl.ds(0, 4), pl.ds(4, 4)
-    up0 = send(keys.at[c, b, lo], up)
-    down1 = send(keys.at[c, b, hi], down)
-    up1 = send(keys.at[c, b, hi], up)
-    down0 = send(keys.at[c, b, lo], down)
-    own = send(keys.at[c, b], twin)
-
-    loads["uk1"].wait()
-    lax.fori_loop(2, 4, qlat, 0)
-
-    prev, nxt, far = (b + 3) % 4, (b + 1) % 4, (b + 2) % 4
-    up0.wait_recv()
-    far0 = send(keys.at[c, prev, lo], up)
-    down1.wait_recv()
-    far1 = send(keys.at[c, nxt, hi], down)
-    up1.wait_recv()
-    t0 = send(keys.at[c, prev], twin)
-    down0.wait_recv()
-    t1 = send(keys.at[c, nxt], twin)
-
-    loads["uk2"].wait()
-    loads["uk3"].wait()
-    lax.fori_loop(4, 8, qlat, 0)
-
-    far0.wait_recv()
-    t2 = send(keys.at[c, far, lo], twin)
-    far1.wait_recv()
-    t3 = send(keys.at[c, far, hi], twin)
-    for copy in doc:
-        copy.wait_recv()
-    for copy in (own, t0, t1, t2, t3):
-        copy.wait_recv()
-    for copy in sent:
-        copy.wait_send()
-
-    for j in range(8):
-        ct[:, j * 128 : (j + 1) * 128] = keys[j // 4, j % 4].reshape(128, WIDE)[:, :LAT].T
-    ct[:, PROMPT:] = docs[...].reshape(128, WIDE)[:, :LAT].T
-    loads["uv"].wait()
+    for j in range(4):
+        loads["uk%d" % j].wait()
+    lax.fori_loop(0, GROUPS, qlat, 0)
 
     key_at = lax.broadcasted_iota(jnp.int32, (TOK, TOK), 0)
     tok_at = lax.broadcasted_iota(jnp.int32, (TOK, TOK), 1)
     causal = jnp.concatenate([key_at <= tok_at] * GROUP, axis=1)
     valid = key_at < ln[0]
-
-    def scores(i, k):
-        top = None
-        for j in range(0, KEYS, 256):
-            if j < PROMPT:
-                block = keys[j // 512, (j // 128) % 4 : (j // 128) % 4 + 2].reshape(256, WIDE)
-                s = dot(block, qt[i])
-            else:
-                s = dot(docs[...].reshape(TOK, WIDE), qt[i])
-                s = jnp.where(causal, s, -1e30)
-            rows = s.shape[0]
-            S[k][j : j + rows] = s
-            m = jnp.max(s.reshape(rows // 8, 8, N), axis=0)
-            top = m if top is None else jnp.maximum(top, m)
-            yield
-        mx[k] = jnp.broadcast_to(jnp.max(top, axis=0, keepdims=True) * SCALE, (8, N))
-        yield
-
-    def weights(k):
-        m = mx[k][:1]
-        total = jnp.zeros((8, N), F32)
-        for r in range(0, KEYS, 64):
-            w = jnp.exp2(S[k][r : r + 64] * SCALE - m)
-            total = total + jnp.sum(w.reshape(8, 8, N), axis=0)
-            PR[k][r : r + 64] = w.astype(BF16)
-            yield
-        inv[k] = jnp.broadcast_to(1.0 / jnp.sum(total, axis=0, keepdims=True), (8, N))
-        yield
-
-    def project(i, k):
-        o = (dot(ct[...], PR[k][...]) * inv[k][:1]).astype(BF16)
-        yield
-        for h in range(GROUP):
-            cols = pl.ds(pl.multiple_of(i * N + h * DV, DV), DV)
-            v = lax.dot_general(
-                o[:, h * TOK : (h + 1) * TOK], uv[:, cols], (((0,), (0,)), ((), ())), preferred_element_type=F32
-            )
-            out_v[:, cols] = jnp.where(valid, v, 0.0).astype(BF16)
-            yield
-        cols = pl.ds(pl.multiple_of(i * N, N), N)
-        pltpu.make_async_copy(out_v.at[:, cols], out_h.at[:, cols], osem.at[i]).start()
-        yield
 
     def run(*steps):
         most = max(n for _, n in steps)
@@ -224,27 +146,135 @@
             for _ in step:
                 pass
 
-    def A(i, k):
-        return scores(i, k), 6
-
-    def B(k):
-        return weights(k), 19
-
-    def C(i, k):
-        return project(i, k), GROUP + 2
-
-    run(A(0, 0))
-    run(A(1, 1), B(0))
-
-    def body(t, _):
-        i = 2 * t + 1
-        run(C(i - 1, 0), A(i + 1, 0), B(1))
-        run(C(i, 1), A(jnp.minimum(i + 2, GROUPS - 1), 1), B(0))
-        return 0
-
-    lax.fori_loop(0, GROUPS // 2 - 1, body, 0)
-    run(C(GROUPS - 2, 0), B(1))
-    run(C(GROUPS - 1, 1))
+    def attend(slabs, at, start, end):
+        rows = len(slabs) * TOK
+        span = slice(at, at + rows)
+
+        def slab(j):
+            if slabs[j] is None:
+                return docs[...].reshape(TOK, WIDE)
+            return keys[slabs[j][0], slabs[j][1]].reshape(TOK, WIDE)
+
+        for j in range(len(slabs)):
+            ct[:, at + j * TOK : at + (j + 1) * TOK] = slab(j)[:, :LAT].T
+
+        def scores(i, k):
+            top = None
+            for j in range(len(slabs)):
+                s = dot(slab(j), qt[i])
+                if slabs[j] is None:
+                    s = jnp.where(causal, s, -1e30)
+                S[k][j * TOK : (j + 1) * TOK] = s
+                m = jnp.max(s.reshape(TOK // 8, 8, N), axis=0)
+                top = m if top is None else jnp.maximum(top, m)
+                yield
+            new = jnp.broadcast_to(jnp.max(top, axis=0, keepdims=True) * SCALE, (8, N))
+            if not start:
+                old = mrun[i]
+                new = jnp.maximum(old, new)
+                al[k] = jnp.exp2(old - new)
+            mx[k] = new
+            if not end:
+                mrun[i] = new
+            yield
+
+        def weights(k):
+            m = mx[k][:1]
+            total = jnp.zeros((8, N), F32)
+            for r in range(0, rows, 64):
+                w = jnp.exp2(S[k][r : r + 64] * SCALE - m)
+                total = total + jnp.sum(w.reshape(8, 8, N), axis=0)
+                PR[k][r : r + 64] = w.astype(BF16)
+                yield
+            sm[k] = total
+            yield
+
+        def project(i, k):
+            total = sm[k]
+            if not start:
+                total = total + lrun[i] * al[k]
+            if not end:
+                lrun[i] = total
+            inverse = 1.0 / jnp.sum(total, axis=0, keepdims=True)
+            parts = []
+            for r in range(0, LAT, 256):
+                o = dot(ct[r : r + 256, span], PR[k][:rows])
+                if not start:
+                    o = o + acc[i, r : r + 256] * al[k][:1]
+                if end:
+                    parts.append((o * inverse).astype(BF16))
+                else:
+                    acc[i, r : r + 256] = o
+                yield
+            if not end:
+                return
+            o = jnp.concatenate(parts, axis=0)
+            for h in range(GROUP):
+                cols = pl.ds(pl.multiple_of(i * N + h * DV, DV), DV)
+                v = lax.dot_general(
+                    o[:, h * TOK : (h + 1) * TOK], uv[:, cols], (((0,), (0,)), ((), ())), preferred_element_type=F32
+                )
+                out_v[:, cols] = jnp.where(valid, v, 0.0).astype(BF16)
+                yield
+            cols = pl.ds(pl.multiple_of(i * N, N), N)
+            pltpu.make_async_copy(out_v.at[:, cols], out_h.at[:, cols], osem.at[i]).start()
+            yield
+
+        def A(i, k):
+            return scores(i, k), len(slabs) + 1
+
+        def B(k):
+            return weights(k), rows // 64 + 1
+
+        def C(i, k):
+            return project(i, k), 2 + (GROUP + 1 if end else 0)
+
+        run(A(0, 0))
+        run(A(1, 1), B(0))
+
+        def body(t, _):
+            i = 2 * t + 1
+            run(C(i - 1, 0), A(i + 1, 0), B(1))
+            run(C(i, 1), A(i + 2, 1), B(0))
+            return 0
+
+        lax.fori_loop(0, GROUPS // 2 - 1, body, 0)
+        run(C(GROUPS - 2, 0), B(1))
+        run(C(GROUPS - 1, 1))
+
+    for copy in first:
+        copy.wait_recv()
+    lo, hi = pl.ds(0, 4), pl.ds(4, 4)
+    up0 = send(keys.at[c, b, lo], up)
+    down1 = send(keys.at[c, b, hi], down)
+    own = send(keys.at[c, b], twin)
+    up1 = send(keys.at[c, b, hi], up)
+    down0 = send(keys.at[c, b, lo], down)
+    own.wait_recv()
+    d = 1 - c
+    attend([(c, b), (d, a)], 0, True, False)
+
+    prev, nxt, far = (b + 3) % 4, (b + 1) % 4, (b + 2) % 4
+    up0.wait_recv()
+    far0 = send(keys.at[c, prev, lo], up)
+    far2 = send(keys.at[c, prev, lo], up_twin)
+    down1.wait_recv()
+    far1 = send(keys.at[c, nxt, hi], down)
+    far3 = send(keys.at[c, nxt, hi], down_twin)
+    up1.wait_recv()
+    t0 = send(keys.at[c, prev], twin)
+    down0.wait_recv()
+    t1 = send(keys.at[c, nxt], twin)
+    for copy in doc:
+        copy.wait_recv()
+    attend([None, (c, prev), (c, nxt)], 256, False, False)
+
+    for copy in (far0, far1, far2, far3, t0, t1):
+        copy.wait_recv()
+    loads["uv"].wait()
+    attend([(d, (a + 3) % 4), (d, (a + 1) % 4), (c, far), (d, (a + 2) % 4)], 640, False, True)
+    for copy in sent:
+        copy.wait_send()
     for i in range(GROUPS):
         cols = pl.ds(i * N, N)
         pltpu.make_async_copy(out_v.at[:, cols], out_h.at[:, cols], osem.at[i]).wait()
@@ -252,7 +282,6 @@
 
 def per_device(q_nope, q_rope, uk_weight, uv_weight, prompt_latent, prompt_rope, doc_latent, doc_rope, doc_lengths):
     hbm = pl.BlockSpec(memory_space=pl.ANY)
-    copies = 20
     return pl.pallas_call(
         kernel,
         out_shape=jax.ShapeDtypeStruct((TOK, HEADS * DV), BF16),
@@ -271,12 +300,16 @@
             pltpu.VMEM((4, 32, WIDE), BF16),
             pltpu.VMEM((LAT, KEYS), BF16),
             pltpu.VMEM((GROUPS, WIDE, N), BF16),
-            pltpu.VMEM((KEYS, N), F32),
-            pltpu.VMEM((KEYS, N), F32),
-            pltpu.VMEM((KEYS, N), BF16),
-            pltpu.VMEM((KEYS, N), BF16),
+            pltpu.VMEM((512, N), F32),
+            pltpu.VMEM((512, N), F32),
+            pltpu.VMEM((512, N), BF16),
+            pltpu.VMEM((512, N), BF16),
             pltpu.VMEM((2, 8, N), F32),
             pltpu.VMEM((2, 8, N), F32),
+            pltpu.VMEM((2, 8, N), F32),
+            pltpu.VMEM((GROUPS, LAT, N), F32),
+            pltpu.VMEM((GROUPS, 8, N), F32),
+            pltpu.VMEM((GROUPS, 8, N), F32),
             pltpu.VMEM((TOK, HEADS * DV), BF16),
             pltpu.SemaphoreType.DMA((11,)),
             pltpu.SemaphoreType.DMA((GROUPS,)),

time: 47 us -> 41.3 us (0.88)
  Pallas kernels: 43.9 us -> 38.2 us
    pallas_call x1, Pallas kernels: 43.9 us -> 38.2 us  [per_device(): pl.pallas_call(kernel, out_shape=jax.ShapeDtypeStruct((TOK, HEADS * DV),...]
where the time goes in v2:
time: 41.3 us; the launch traced here: 41.2 us
  Pallas kernels  38.2 us (92%)
  local copies, waits for them, and re-layouts  2.29 us (6%)
  between operations  0.66 us (2%)
    pallas_call x1, Pallas kernels, per_device(): pl.pallas_call(kernel, out_shape=jax.ShapeDtypeStruct((TOK, HEADS * DV),...  38.2 us
    unnamed x1, local copies, waits for them, and re-layouts  2.29 us

profile of v2, /device:TPU:1, one launch (start us, length us, event | category | flops | bytes accessed | tf_op | source)
XLA Modules:
  0.0 41.2 jit_solution(9093453146513586170)
XLA Ops:
  0.7 38.2 %attend.1 = bf16[128,4096]{1,0:T(8,128)(2,1)} custom-call(bf16[128,4096]{1,0:T(8,128)(2,1)} %qn_h.1, bf16[128,2048]{1,0:T(8,128)(2,1)} %qr_h.1, bf16[512,4096]{1,0:T(8,128)(2,1)} %uk_h.1, bf16[512,4096]{1,0:T(8,128)(2,1)} %uv_h.1, bf16[16,512]{1,0:T(8,128)(2,1)} %pl_h.1, bf16[16,64]{1,0:T(8,128)(2,1)} %pr_h.1, bf16[32,512]{1,0:T(8,128)(2,1)} %dl_h.1, ...), custom_call_target="tpu_custom_call" | custom-call | tf_op jit(solution)/shard_map/attend/pallas_call | solution.py:285
  38.9 2.3 %copy.12 = bf16[128,4096]{1,0:T(8,128)(2,1)} copy(bf16[128,4096]{1,0:T(8,128)(2,1)} %attend.1) | data formatting | bytes 2097152

commit v3 on v2

--- a/solution.py
+++ b/solution.py
@@ -52,13 +52,14 @@
 
     flip = 1 - 2 * c
     near = [(place(b, (g + d) % 8), ten) for d in range(1, 8)]
-    up_at, down_at = place((b + 1) % 4, g), place((b + 3) % 4, g)
-    up, down = (up_at, ten), (down_at, ten)
-    up_twin, down_twin = (up_at + flip, ten), (down_at + flip, ten)
-    v_up = (c * ((x + 1) % 4) + (1 - c) * x) * 16 + (c * y + (1 - c) * ((y + 1) % 4)) * 4 + zl * 2 + (1 - c)
-    v_down = (c * ((x + 3) % 4) + (1 - c) * x) * 16 + (c * y + (1 - c) * ((y + 3) % 4)) * 4 + zl * 2 + (1 - c)
+    up, down = (place((b + 1) % 4, g), ten), (place((b + 3) % 4, g), ten)
+    far_at = place((b + 2) % 4, g)
+    far, far_twin = (far_at, ten), (far_at + flip, ten)
+    v_x = c * ((x + 2) % 4) + (1 - c) * x
+    v_y = c * y + (1 - c) * ((y + 2) % 4)
+    v_far = (v_x * 16 + v_y * 4 + zl * 2 + 1 - c, ten)
     twin = (me + flip, ten)
-    others = [(me, (ten + d) % 4) for d in range(1, 4)]
+    t_up, t_down = (me, (ten + 1) % 4), (me, (ten + 3) % 4)
 
     loads = {}
 
@@ -77,7 +78,7 @@
     load("uv", uv_h, uv, 10)
 
     barrier = pltpu.get_barrier_semaphore()
-    peers = near + [up, down, up_twin, down_twin, (v_up, ten), (v_down, ten), twin] + others
+    peers = near + [up, down, far, far_twin, v_far, twin, t_up, t_down]
     for peer in peers:
         pl.semaphore_signal(barrier, inc=1, device_id=peer, device_id_type=MESH)
 
@@ -103,7 +104,7 @@
         return copy
 
     first = [send(keys.at[c, b, g], peer) for peer in near]
-    doc = [send(docs.at[ten], peer) for peer in others]
+    doc_up, doc_down = send(docs.at[ten], t_up), send(docs.at[ten], t_down)
 
     def qlat(i, _):
         zero = jnp.zeros((TOK, TOK), BF16)
@@ -127,7 +128,7 @@
     loads["qr"].wait()
     for j in range(4):
         loads["uk%d" % j].wait()
-    lax.fori_loop(0, GROUPS, qlat, 0)
+        lax.fori_loop(2 * j, 2 * j + 2, qlat, 0)
 
     key_at = lax.broadcasted_iota(jnp.int32, (TOK, TOK), 0)
     tok_at = lax.broadcasted_iota(jnp.int32, (TOK, TOK), 1)
@@ -160,13 +161,17 @@
 
         def scores(i, k):
             top = None
-            for j in range(len(slabs)):
-                s = dot(slab(j), qt[i])
-                if slabs[j] is None:
-                    s = jnp.where(causal, s, -1e30)
-                S[k][j * TOK : (j + 1) * TOK] = s
-                m = jnp.max(s.reshape(TOK // 8, 8, N), axis=0)
-                top = m if top is None else jnp.maximum(top, m)
+            step = 4
+            for j in range(0, len(slabs), step):
+                some = slabs[j : j + step]
+                s = dot(jnp.concatenate([slab(j + n) for n in range(len(some))], axis=0), qt[i])
+                for n, which in enumerate(some):
+                    part = s[n * TOK : (n + 1) * TOK]
+                    if which is None:
+                        part = jnp.where(causal, part, -1e30)
+                    S[k][(j + n) * TOK : (j + n + 1) * TOK] = part
+                    m = jnp.max(part.reshape(TOK // 8, 8, N), axis=0)
+                    top = m if top is None else jnp.maximum(top, m)
                 yield
             new = jnp.broadcast_to(jnp.max(top, axis=0, keepdims=True) * SCALE, (8, N))
             if not start:
@@ -192,19 +197,20 @@
         def project(i, k):
             total = sm[k]
             if not start:
-                total = total + lrun[i] * al[k]
+                fade = al[k]
+                total = total + lrun[i] * fade
             if not end:
                 lrun[i] = total
             inverse = 1.0 / jnp.sum(total, axis=0, keepdims=True)
             parts = []
-            for r in range(0, LAT, 256):
-                o = dot(ct[r : r + 256, span], PR[k][:rows])
+            for r in range(0, LAT, 512):
+                o = dot(ct[r : r + 512, span], PR[k][:rows])
                 if not start:
-                    o = o + acc[i, r : r + 256] * al[k][:1]
+                    o = o + acc[i, r : r + 512] * fade[:1]
                 if end:
                     parts.append((o * inverse).astype(BF16))
                 else:
-                    acc[i, r : r + 256] = o
+                    acc[i, r : r + 512] = o
                 yield
             if not end:
                 return
@@ -221,58 +227,64 @@
             yield
 
         def A(i, k):
-            return scores(i, k), len(slabs) + 1
+            return scores(i, k), -(-len(slabs) // 4) + 1
 
         def B(k):
             return weights(k), rows // 64 + 1
 
         def C(i, k):
-            return project(i, k), 2 + (GROUP + 1 if end else 0)
-
-        run(A(0, 0))
-        run(A(1, 1), B(0))
+            return project(i, k), 1 + (GROUP + 1 if end else 0)
+
+        return A, B, C
+
+    def loop(stages):
+        A, B, C = stages
 
         def body(t, _):
             i = 2 * t + 1
-            run(C(i - 1, 0), A(i + 1, 0), B(1))
-            run(C(i, 1), A(i + 2, 1), B(0))
+            run(A(i + 1, 0), B(1), C(i - 1, 0))
+            run(A(i + 2, 1), B(0), C(i, 1))
             return 0
 
         lax.fori_loop(0, GROUPS // 2 - 1, body, 0)
-        run(C(GROUPS - 2, 0), B(1))
-        run(C(GROUPS - 1, 1))
+
+    def join(old, new):
+        run(new[0](0, 0), old[1](1), old[2](GROUPS - 2, 0))
+        run(new[0](1, 1), new[1](0), old[2](GROUPS - 1, 1))
 
     for copy in first:
         copy.wait_recv()
-    lo, hi = pl.ds(0, 4), pl.ds(4, 4)
-    up0 = send(keys.at[c, b, lo], up)
-    down1 = send(keys.at[c, b, hi], down)
     own = send(keys.at[c, b], twin)
-    up1 = send(keys.at[c, b, hi], up)
-    down0 = send(keys.at[c, b, lo], down)
+    up0, down0 = send(keys.at[c, b], up), send(keys.at[c, b], down)
+    prev, nxt, opp, d = (b + 3) % 4, (b + 1) % 4, (b + 2) % 4, 1 - c
+    doc_up.wait_recv()
+    doc_far0 = send(docs.at[(ten + 3) % 4, pl.ds(0, 16)], t_up)
+    doc_down.wait_recv()
+    doc_far1 = send(docs.at[(ten + 1) % 4, pl.ds(16, 16)], t_down)
     own.wait_recv()
-    d = 1 - c
-    attend([(c, b), (d, a)], 0, True, False)
-
-    prev, nxt, far = (b + 3) % 4, (b + 1) % 4, (b + 2) % 4
+    one = attend([(c, b), (d, a)], 0, True, False)
+    run(one[0](0, 0))
+    run(one[0](1, 1), one[1](0))
+    loop(one)
+
     up0.wait_recv()
-    far0 = send(keys.at[c, prev, lo], up)
-    far2 = send(keys.at[c, prev, lo], up_twin)
-    down1.wait_recv()
-    far1 = send(keys.at[c, nxt, hi], down)
-    far3 = send(keys.at[c, nxt, hi], down_twin)
-    up1.wait_recv()
-    t0 = send(keys.at[c, prev], twin)
     down0.wait_recv()
-    t1 = send(keys.at[c, nxt], twin)
-    for copy in doc:
-        copy.wait_recv()
-    attend([None, (c, prev), (c, nxt)], 256, False, False)
-
-    for copy in (far0, far1, far2, far3, t0, t1):
+    t0, t1 = send(keys.at[c, prev], twin), send(keys.at[c, nxt], twin)
+    far0, far1 = send(keys.at[c, b], far), send(keys.at[c, b], far_twin)
+    doc_far0.wait_recv()
+    doc_far1.wait_recv()
+    two = attend([None, (c, prev), (c, nxt)], 256, False, False)
+    join(one, two)
+    loop(two)
+
+    for copy in (far0, far1, t0, t1):
         copy.wait_recv()
     loads["uv"].wait()
-    attend([(d, (a + 3) % 4), (d, (a + 1) % 4), (c, far), (d, (a + 2) % 4)], 640, False, True)
+    three = attend([(d, (a + 3) % 4), (d, (a + 1) % 4), (c, opp), (d, (a + 2) % 4)], 640, False, True)
+    join(two, three)
+    loop(three)
+    run(three[2](GROUPS - 2, 0), three[1](1))
+    run(three[2](GROUPS - 1, 1))
     for copy in sent:
         copy.wait_send()
     for i in range(GROUPS):

time: 41.3 us -> 40.8 us (0.988)
  Pallas kernels: 38.2 us -> 37.7 us
    pallas_call x1, Pallas kernels: 38.2 us -> 37.7 us  [per_device(): pl.pallas_call(kernel, out_shape=jax.ShapeDtypeStruct((TOK, HEADS * DV),...]
where the time goes in v3:
time: 40.8 us; the launch traced here: 40.6 us
  Pallas kernels  37.7 us (92%)
  local copies, waits for them, and re-layouts  2.29 us (6%)
  between operations  0.66 us (2%)
    pallas_call x1, Pallas kernels, per_device(): pl.pallas_call(kernel, out_shape=jax.ShapeDtypeStruct((TOK, HEADS * DV),...  37.7 us
    unnamed x1, local copies, waits for them, and re-layouts  2.29 us

profile of v3, /device:TPU:1, one launch (start us, length us, event | category | flops | bytes accessed | tf_op | source)
XLA Modules:
  0.0 40.6 jit_solution(10475629163641737972)
XLA Ops:
  0.7 37.7 %attend.1 = bf16[128,4096]{1,0:T(8,128)(2,1)} custom-call(bf16[128,4096]{1,0:T(8,128)(2,1)} %qn_h.1, bf16[128,2048]{1,0:T(8,128)(2,1)} %qr_h.1, bf16[512,4096]{1,0:T(8,128)(2,1)} %uk_h.1, bf16[512,4096]{1,0:T(8,128)(2,1)} %uv_h.1, bf16[16,512]{1,0:T(8,128)(2,1)} %pl_h.1, bf16[16,64]{1,0:T(8,128)(2,1)} %pr_h.1, bf16[32,512]{1,0:T(8,128)(2,1)} %dl_h.1, ...), custom_call_target="tpu_custom_call" | custom-call | tf_op jit(solution)/shard_map/attend/pallas_call | solution.py:297
  38.4 2.3 %copy.12 = bf16[128,4096]{1,0:T(8,128)(2,1)} copy(bf16[128,4096]{1,0:T(8,128)(2,1)} %attend.1) | data formatting | bytes 2097152

commit v4 on v3

--- a/solution.py
+++ b/solution.py
@@ -51,7 +51,11 @@
         return x_ * 16 + y_ * 4 + z_ * 2 + c
 
     flip = 1 - 2 * c
-    near = [(place(b, (g + d) % 8), ten) for d in range(1, 8)]
+    near = []
+    for d in range(1, 8):
+        at = (g + d) % 8
+        cross = (at + zl) % 2 * ((at // 2 + a) % 2)
+        near.append((place(b, at), (ten + cross * (3 - 2 * zl)) % 4))
     up, down = (place((b + 1) % 4, g), ten), (place((b + 3) % 4, g), ten)
     far_at = place((b + 2) % 4, g)
     far, far_twin = (far_at, ten), (far_at + flip, ten)
@@ -93,18 +97,21 @@
     count = [0]
     sent = []
 
-    def send(ref, peer):
+    def cross_copy(ref, peer):
         k = count[0]
         count[0] += 1
         copy = pltpu.make_async_remote_copy(
             src_ref=ref, dst_ref=ref, send_sem=ssem.at[k], recv_sem=rsem.at[k], device_id=peer, device_id_type=MESH
         )
-        copy.start()
         sent.append(copy)
         return copy
 
+    def send(ref, peer):
+        copy = cross_copy(ref, peer)
+        copy.start()
+        return copy
+
     first = [send(keys.at[c, b, g], peer) for peer in near]
-    doc_up, doc_down = send(docs.at[ten], t_up), send(docs.at[ten], t_down)
 
     def qlat(i, _):
         zero = jnp.zeros((TOK, TOK), BF16)
@@ -118,9 +125,9 @@
                 ],
                 axis=0,
             )
-            qt[i, :LAT, p * 256 : (p + 1) * 256] = dot(uk[:, cols], diag).astype(BF16)
+            qt[i, :LAT, p * 256 : (p + 1) * 256] = (dot(uk[:, cols], diag) * SCALE).astype(BF16)
             r = qr[:, pl.ds(pl.multiple_of(i * (N // 2) + p * 128, 128), 128)].T
-            qt[i, LAT : LAT + DR, p * 256 : (p + 1) * 256] = jnp.concatenate([r[:DR], r[DR:]], axis=1)
+            qt[i, LAT : LAT + DR, p * 256 : (p + 1) * 256] = (jnp.concatenate([r[:DR], r[DR:]], axis=1).astype(F32) * SCALE).astype(BF16)
         qt[i, LAT + DR :, :] = jnp.zeros((WIDE - LAT - DR, N), BF16)
         return 0
 
@@ -161,7 +168,7 @@
 
         def scores(i, k):
             top = None
-            step = 4
+            step = 5
             for j in range(0, len(slabs), step):
                 some = slabs[j : j + step]
                 s = dot(jnp.concatenate([slab(j + n) for n in range(len(some))], axis=0), qt[i])
@@ -173,7 +180,7 @@
                     m = jnp.max(part.reshape(TOK // 8, 8, N), axis=0)
                     top = m if top is None else jnp.maximum(top, m)
                 yield
-            new = jnp.broadcast_to(jnp.max(top, axis=0, keepdims=True) * SCALE, (8, N))
+            new = jnp.broadcast_to(jnp.max(top, axis=0, keepdims=True), (8, N))
             if not start:
                 old = mrun[i]
                 new = jnp.maximum(old, new)
@@ -187,7 +194,7 @@
             m = mx[k][:1]
             total = jnp.zeros((8, N), F32)
             for r in range(0, rows, 64):
-                w = jnp.exp2(S[k][r : r + 64] * SCALE - m)
+                w = jnp.exp2(S[k][r : r + 64] - m)
                 total = total + jnp.sum(w.reshape(8, 8, N), axis=0)
                 PR[k][r : r + 64] = w.astype(BF16)
                 yield
@@ -227,7 +234,7 @@
             yield
 
         def A(i, k):
-            return scores(i, k), -(-len(slabs) // 4) + 1
+            return scores(i, k), -(-len(slabs) // 5) + 1
 
         def B(k):
             return weights(k), rows // 64 + 1
@@ -237,11 +244,13 @@
 
         return A, B, C
 
-    def loop(stages):
+    def loop(stages, extra=None):
         A, B, C = stages
 
         def body(t, _):
             i = 2 * t + 1
+            if extra is not None:
+                pl.when(t == 1)(extra)
             run(A(i + 1, 0), B(1), C(i - 1, 0))
             run(A(i + 2, 1), B(0), C(i, 1))
             return 0
@@ -257,30 +266,38 @@
     own = send(keys.at[c, b], twin)
     up0, down0 = send(keys.at[c, b], up), send(keys.at[c, b], down)
     prev, nxt, opp, d = (b + 3) % 4, (b + 1) % 4, (b + 2) % 4, 1 - c
+    doc_up, doc_down = send(docs.at[ten], t_up), send(docs.at[ten], t_down)
+    own.wait_recv()
+    crossing = [cross_copy(keys.at[c, b], peer) for peer in (far, far_twin)]
+
+    def cross_over():
+        for copy in (up0, down0):
+            copy.wait_send()
+        sent[:] = [copy for copy in sent if copy is not up0 and copy is not down0]
+        for copy in crossing:
+            copy.start()
+
+    one = attend([(c, b), (d, a)], 0, True, False)
+    run(one[0](0, 0))
+    run(one[0](1, 1), one[1](0))
+    loop(one, cross_over)
+    far0, far1 = crossing
     doc_up.wait_recv()
     doc_far0 = send(docs.at[(ten + 3) % 4, pl.ds(0, 16)], t_up)
     doc_down.wait_recv()
     doc_far1 = send(docs.at[(ten + 1) % 4, pl.ds(16, 16)], t_down)
-    own.wait_recv()
-    one = attend([(c, b), (d, a)], 0, True, False)
-    run(one[0](0, 0))
-    run(one[0](1, 1), one[1](0))
-    loop(one)
 
     up0.wait_recv()
     down0.wait_recv()
     t0, t1 = send(keys.at[c, prev], twin), send(keys.at[c, nxt], twin)
-    far0, far1 = send(keys.at[c, b], far), send(keys.at[c, b], far_twin)
-    doc_far0.wait_recv()
-    doc_far1.wait_recv()
-    two = attend([None, (c, prev), (c, nxt)], 256, False, False)
+    two = attend([(c, prev), (c, nxt)], 256, False, False)
     join(one, two)
     loop(two)
 
-    for copy in (far0, far1, t0, t1):
+    for copy in (doc_far0, doc_far1, far0, far1, t0, t1):
         copy.wait_recv()
     loads["uv"].wait()
-    three = attend([(d, (a + 3) % 4), (d, (a + 1) % 4), (c, opp), (d, (a + 2) % 4)], 640, False, True)
+    three = attend([None, (d, (a + 3) % 4), (d, (a + 1) % 4), (c, opp), (d, (a + 2) % 4)], 512, False, True)
     join(two, three)
     loop(three)
     run(three[2](GROUPS - 2, 0), three[1](1))
@@ -312,10 +329,10 @@
             pltpu.VMEM((4, 32, WIDE), BF16),
             pltpu.VMEM((LAT, KEYS), BF16),
             pltpu.VMEM((GROUPS, WIDE, N), BF16),
-            pltpu.VMEM((512, N), F32),
-            pltpu.VMEM((512, N), F32),
-            pltpu.VMEM((512, N), BF16),
-            pltpu.VMEM((512, N), BF16),
+            pltpu.VMEM((640, N), F32),
+            pltpu.VMEM((640, N), F32),
+            pltpu.VMEM((640, N), BF16),
+            pltpu.VMEM((640, N), BF16),
             pltpu.VMEM((2, 8, N), F32),
             pltpu.VMEM((2, 8, N), F32),
             pltpu.VMEM((2, 8, N), F32),

time: 40.8 us -> 40.1 us (0.983)
  Pallas kernels: 37.7 us -> 37 us
    pallas_call x1, Pallas kernels: 37.7 us -> 37 us  [per_device(): pl.pallas_call(kernel, out_shape=jax.ShapeDtypeStruct((TOK, HEADS * DV),...]
where the time goes in v4:
time: 40.1 us; the launch traced here: 40 us
  Pallas kernels  37 us (92%)
  local copies, waits for them, and re-layouts  2.29 us (6%)
  between operations  0.66 us (2%)
    pallas_call x1, Pallas kernels, per_device(): pl.pallas_call(kernel, out_shape=jax.ShapeDtypeStruct((TOK, HEADS * DV),...  37 us
    unnamed x1, local copies, waits for them, and re-layouts  2.29 us

profile of v4, /device:TPU:1, one launch (start us, length us, event | category | flops | bytes accessed | tf_op | source)
XLA Modules:
  0.0 40.0 jit_solution(10180455098557604681)
XLA Ops:
  0.7 37.0 %attend.1 = bf16[128,4096]{1,0:T(8,128)(2,1)} custom-call(bf16[128,4096]{1,0:T(8,128)(2,1)} %qn_h.1, bf16[128,2048]{1,0:T(8,128)(2,1)} %qr_h.1, bf16[512,4096]{1,0:T(8,128)(2,1)} %uk_h.1, bf16[512,4096]{1,0:T(8,128)(2,1)} %uv_h.1, bf16[16,512]{1,0:T(8,128)(2,1)} %pl_h.1, bf16[16,64]{1,0:T(8,128)(2,1)} %pr_h.1, bf16[32,512]{1,0:T(8,128)(2,1)} %dl_h.1, ...), custom_call_target="tpu_custom_call" | custom-call | tf_op jit(solution)/shard_map/attend/pallas_call | solution.py:314
  37.7 2.3 %copy.12 = bf16[128,4096]{1,0:T(8,128)(2,1)} copy(bf16[128,4096]{1,0:T(8,128)(2,1)} %attend.1) | data formatting | bytes 2097152

commit v5 on v4

--- a/solution.py
+++ b/solution.py
@@ -17,7 +17,7 @@
 WIDE = 640
 TOK = 128
 HEADS = 32
-GROUP = 4
+GROUP = 8
 N = GROUP * TOK
 GROUPS = HEADS // GROUP
 PROMPT = 1024
@@ -125,9 +125,9 @@
                 ],
                 axis=0,
             )
-            qt[i, :LAT, p * 256 : (p + 1) * 256] = (dot(uk[:, cols], diag) * SCALE).astype(BF16)
+            qt[i, :LAT, p * 256 : (p + 1) * 256] = dot(uk[:, cols], diag).astype(BF16)
             r = qr[:, pl.ds(pl.multiple_of(i * (N // 2) + p * 128, 128), 128)].T
-            qt[i, LAT : LAT + DR, p * 256 : (p + 1) * 256] = (jnp.concatenate([r[:DR], r[DR:]], axis=1).astype(F32) * SCALE).astype(BF16)
+            qt[i, LAT : LAT + DR, p * 256 : (p + 1) * 256] = jnp.concatenate([r[:DR], r[DR:]], axis=1)
         qt[i, LAT + DR :, :] = jnp.zeros((WIDE - LAT - DR, N), BF16)
         return 0
 
@@ -135,7 +135,7 @@
     loads["qr"].wait()
     for j in range(4):
         loads["uk%d" % j].wait()
-        lax.fori_loop(2 * j, 2 * j + 2, qlat, 0)
+        lax.fori_loop(GROUPS * j // 4, GROUPS * (j + 1) // 4, qlat, 0)
 
     key_at = lax.broadcasted_iota(jnp.int32, (TOK, TOK), 0)
     tok_at = lax.broadcasted_iota(jnp.int32, (TOK, TOK), 1)
@@ -180,7 +180,7 @@
                     m = jnp.max(part.reshape(TOK // 8, 8, N), axis=0)
                     top = m if top is None else jnp.maximum(top, m)
                 yield
-            new = jnp.broadcast_to(jnp.max(top, axis=0, keepdims=True), (8, N))
+            new = jnp.broadcast_to(jnp.max(top, axis=0, keepdims=True) * SCALE, (8, N))
             if not start:
                 old = mrun[i]
                 new = jnp.maximum(old, new)
@@ -194,7 +194,7 @@
             m = mx[k][:1]
             total = jnp.zeros((8, N), F32)
             for r in range(0, rows, 64):
-                w = jnp.exp2(S[k][r : r + 64] - m)
+                w = jnp.exp2(S[k][r : r + 64] * SCALE - m)
                 total = total + jnp.sum(w.reshape(8, 8, N), axis=0)
                 PR[k][r : r + 64] = w.astype(BF16)
                 yield
@@ -250,7 +250,7 @@
         def body(t, _):
             i = 2 * t + 1
             if extra is not None:
-                pl.when(t == 1)(extra)
+                pl.when(t == 0)(extra)
             run(A(i + 1, 0), B(1), C(i - 1, 0))
             run(A(i + 2, 1), B(0), C(i, 1))
             return 0

time: 40.1 us -> 39.8 us (level)
  no operation moved by 1% of the time
where the time goes in v5:
time: 39.8 us; the launch traced here: 39.6 us
  Pallas kernels  36.6 us (92%)
  local copies, waits for them, and re-layouts  2.29 us (6%)
  between operations  0.66 us (2%)
    pallas_call x1, Pallas kernels, per_device(): pl.pallas_call(kernel, out_shape=jax.ShapeDtypeStruct((TOK, HEADS * DV),...  36.6 us
    unnamed x1, local copies, waits for them, and re-layouts  2.29 us

profile of v5, /device:TPU:1, one launch (start us, length us, event | category | flops | bytes accessed | tf_op | source)
XLA Modules:
  0.0 39.6 jit_solution(16203077122928404822)
XLA Ops:
  0.7 36.6 %attend.1 = bf16[128,4096]{1,0:T(8,128)(2,1)} custom-call(bf16[128,4096]{1,0:T(8,128)(2,1)} %qn_h.1, bf16[128,2048]{1,0:T(8,128)(2,1)} %qr_h.1, bf16[512,4096]{1,0:T(8,128)(2,1)} %uk_h.1, bf16[512,4096]{1,0:T(8,128)(2,1)} %uv_h.1, bf16[16,512]{1,0:T(8,128)(2,1)} %pl_h.1, bf16[16,64]{1,0:T(8,128)(2,1)} %pr_h.1, bf16[32,512]{1,0:T(8,128)(2,1)} %dl_h.1, ...), custom_call_target="tpu_custom_call" | custom-call | tf_op jit(solution)/shard_map/attend/pallas_call | solution.py:314
  37.3 2.3 %copy.12 = bf16[128,4096]{1,0:T(8,128)(2,1)} copy(bf16[128,4096]{1,0:T(8,128)(2,1)} %attend.1) | data formatting | bytes 2097152

commit v6 on v5

--- a/solution.py
+++ b/solution.py
@@ -210,14 +210,14 @@
                 lrun[i] = total
             inverse = 1.0 / jnp.sum(total, axis=0, keepdims=True)
             parts = []
-            for r in range(0, LAT, 512):
-                o = dot(ct[r : r + 512, span], PR[k][:rows])
+            for r in range(0, LAT, 256):
+                o = dot(ct[r : r + 256, span], PR[k][:rows])
                 if not start:
-                    o = o + acc[i, r : r + 512] * fade[:1]
+                    o = o + acc[i, r : r + 256] * fade[:1]
                 if end:
                     parts.append((o * inverse).astype(BF16))
                 else:
-                    acc[i, r : r + 512] = o
+                    acc[i, r : r + 256] = o
                 yield
             if not end:
                 return
@@ -240,7 +240,7 @@
             return weights(k), rows // 64 + 1
 
         def C(i, k):
-            return project(i, k), 1 + (GROUP + 1 if end else 0)
+            return project(i, k), 2 + (GROUP + 1 if end else 0)
 
         return A, B, C
 
@@ -294,14 +294,20 @@
     join(one, two)
     loop(two)
 
-    for copy in (doc_far0, doc_far1, far0, far1, t0, t1):
+    for copy in (doc_far0, doc_far1, t0, t1):
+        copy.wait_recv()
+    three = attend([None, (d, (a + 3) % 4), (d, (a + 1) % 4)], 512, False, False)
+    join(two, three)
+    loop(three)
+
+    for copy in (far0, far1):
         copy.wait_recv()
     loads["uv"].wait()
-    three = attend([None, (d, (a + 3) % 4), (d, (a + 1) % 4), (c, opp), (d, (a + 2) % 4)], 512, False, True)
-    join(two, three)
-    loop(three)
-    run(three[2](GROUPS - 2, 0), three[1](1))
-    run(three[2](GROUPS - 1, 1))
+    four = attend([(c, opp), (d, (a + 2) % 4)], 896, False, True)
+    join(three, four)
+    loop(four)
+    run(four[2](GROUPS - 2, 0), four[1](1))
+    run(four[2](GROUPS - 1, 1))
     for copy in sent:
         copy.wait_send()
     for i in range(GROUPS):
@@ -329,10 +335,10 @@
             pltpu.VMEM((4, 32, WIDE), BF16),
             pltpu.VMEM((LAT, KEYS), BF16),
             pltpu.VMEM((GROUPS, WIDE, N), BF16),
-            pltpu.VMEM((640, N), F32),
-            pltpu.VMEM((640, N), F32),
-            pltpu.VMEM((640, N), BF16),
-            pltpu.VMEM((640, N), BF16),
+            pltpu.VMEM((384, N), F32),
+            pltpu.VMEM((384, N), F32),
+            pltpu.VMEM((384, N), BF16),
+            pltpu.VMEM((384, N), BF16),
             pltpu.VMEM((2, 8, N), F32),
             pltpu.VMEM((2, 8, N), F32),
             pltpu.VMEM((2, 8, N), F32),

time: 39.8 us -> 38.6 us (0.970)
  Pallas kernels: 36.6 us -> 35.5 us
    pallas_call x1, Pallas kernels: 36.6 us -> 35.5 us  [per_device(): pl.pallas_call(kernel, out_shape=jax.ShapeDtypeStruct((TOK, HEADS * DV),...]
where the time goes in v6:
time: 38.6 us; the launch traced here: 38.4 us
  Pallas kernels  35.5 us (92%)
  local copies, waits for them, and re-layouts  2.29 us (6%)
  between operations  0.66 us (2%)
    pallas_call x1, Pallas kernels, per_device(): pl.pallas_call(kernel, out_shape=jax.ShapeDtypeStruct((TOK, HEADS * DV),...  35.5 us
    unnamed x1, local copies, waits for them, and re-layouts  2.29 us

profile of v6, /device:TPU:1, one launch (start us, length us, event | category | flops | bytes accessed | tf_op | source)
XLA Modules:
  0.0 38.4 jit_solution(12974011757128161761)
XLA Ops:
  0.7 35.5 %attend.1 = bf16[128,4096]{1,0:T(8,128)(2,1)} custom-call(bf16[128,4096]{1,0:T(8,128)(2,1)} %qn_h.1, bf16[128,2048]{1,0:T(8,128)(2,1)} %qr_h.1, bf16[512,4096]{1,0:T(8,128)(2,1)} %uk_h.1, bf16[512,4096]{1,0:T(8,128)(2,1)} %uv_h.1, bf16[16,512]{1,0:T(8,128)(2,1)} %pl_h.1, bf16[16,64]{1,0:T(8,128)(2,1)} %pr_h.1, bf16[32,512]{1,0:T(8,128)(2,1)} %dl_h.1, ...), custom_call_target="tpu_custom_call" | custom-call | tf_op jit(solution)/shard_map/attend/pallas_call | solution.py:320
  36.1 2.3 %copy.12 = bf16[128,4096]{1,0:T(8,128)(2,1)} copy(bf16[128,4096]{1,0:T(8,128)(2,1)} %attend.1) | data formatting | bytes 2097152

commit v7 on v6

--- a/solution.py
+++ b/solution.py
@@ -51,11 +51,7 @@
         return x_ * 16 + y_ * 4 + z_ * 2 + c
 
     flip = 1 - 2 * c
-    near = []
-    for d in range(1, 8):
-        at = (g + d) % 8
-        cross = (at + zl) % 2 * ((at // 2 + a) % 2)
-        near.append((place(b, at), (ten + cross * (3 - 2 * zl)) % 4))
+    near = [(place(b, (g + d) % 8), ten) for d in range(1, 8)]
     up, down = (place((b + 1) % 4, g), ten), (place((b + 3) % 4, g), ten)
     far_at = place((b + 2) % 4, g)
     far, far_twin = (far_at, ten), (far_at + flip, ten)

time: 38.6 us -> 38.5 us (level)
  no operation moved by 1% of the time
where the time goes in v7:
time: 38.5 us; the launch traced here: 38.3 us
  Pallas kernels  35.4 us (92%)
  local copies, waits for them, and re-layouts  2.29 us (6%)
  between operations  0.66 us (2%)
    pallas_call x1, Pallas kernels, per_device(): pl.pallas_call(kernel, out_shape=jax.ShapeDtypeStruct((TOK, HEADS * DV),...  35.4 us
    unnamed x1, local copies, waits for them, and re-layouts  2.29 us

profile of v7, /device:TPU:1, one launch (start us, length us, event | category | flops | bytes accessed | tf_op | source)
XLA Modules:
  0.0 38.3 jit_solution(8097586549412894711)
XLA Ops:
  0.7 35.4 %attend.1 = bf16[128,4096]{1,0:T(8,128)(2,1)} custom-call(bf16[128,4096]{1,0:T(8,128)(2,1)} %qn_h.1, bf16[128,2048]{1,0:T(8,128)(2,1)} %qr_h.1, bf16[512,4096]{1,0:T(8,128)(2,1)} %uk_h.1, bf16[512,4096]{1,0:T(8,128)(2,1)} %uv_h.1, bf16[16,512]{1,0:T(8,128)(2,1)} %pl_h.1, bf16[16,64]{1,0:T(8,128)(2,1)} %pr_h.1, bf16[32,512]{1,0:T(8,128)(2,1)} %dl_h.1, ...), custom_call_target="tpu_custom_call" | custom-call | tf_op jit(solution)/shard_map/attend/pallas_call | solution.py:316
  36.0 2.3 %copy.12 = bf16[128,4096]{1,0:T(8,128)(2,1)} copy(bf16[128,4096]{1,0:T(8,128)(2,1)} %attend.1) | data formatting | bytes 2097152
